TPU v7x, 512 devices: a whole 4x8x8 slice. The times are simulated.
512 devices in a mesh: users: 64 (over z, x, core), ctx: 8 (over y).
Axes of the slice: x: 4, y: 8, z: 8, core: 2. Of those that a mesh axis runs over, the one named last changes fastest.
Arguments:
- events: bfloat16 [32768, 1024], P(('users', 'ctx')), may hold values from -6 to 6
- owner_id: int32 [32768, 1], P(('users', 'ctx')), may hold values from 0 to 63; in each aligned block of 64 rows (0 to 63, 64 to 127, ...) at most 2 rows name the same one
- event_bucket: int32 [32768], P(('users', 'ctx')), may hold values from 0 to 31
- cross_weight: bfloat16 [1024, 1024], P('users'), may hold values from -0.1875 to 0.1875
- cross_bias: float32 [1024], replicated, may hold values from -3 to 3
- project_weight: bfloat16 [1024, 4096], P('users'), may hold values from -0.1875 to 0.1875
- cache_keys: bfloat16 [64, 8192, 1024], P('users', 'ctx'), may hold values from -6 to 6
- cache_values: bfloat16 [64, 8192, 1024], P('users', 'ctx'), may hold values from -60 to 60
- cache_length: int32 [64], P('users'), may hold values from 1024 to 8192
- cache_bucket: int32 [64, 8192], P('users', 'ctx'), may hold values from 0 to 31
- time_bias: float32 [32, 8], replicated, may hold values from -3 to 3
- norm_gain: float32 [1024], replicated, may hold values from 0.1 to 1.9
Outputs:
- gated: bfloat16 [32768, 1024], P(('users', 'ctx'))
Inputs may be any that keep to these rules, and one draw needn't show every extreme that they name: `owner_id`: no user is named by more than 2 of the 64 rows of one ingestion shard, and some user reaches that.
All inputs are finite; a program needn't handle non-finite values.
Results may differ from a plain program's by a relative error of at most 0.035.
Values may be sent and summed in bfloat16 or wider, within the bound.
A program may use at most 64 MiB of HBM per device.

v0:
```python
import jax
import jax.numpy as jnp
from jax import lax
from jax.sharding import PartitionSpec as P

H = 8
norm_epsilon = 1e-05


def from_everyone(value, axis):
    copies = jnp.broadcast_to(value, (lax.axis_size(axis), *value.shape))
    return lax.all_to_all(copies, axis, split_axis=0, concat_axis=0, tiled=True)


def in_order(parts, dim):
    parts = jnp.moveaxis(parts, 0, dim)
    dims = parts.shape
    return parts.reshape(*dims[:dim], dims[dim] * dims[dim + 1], *dims[dim + 2 :])


def gather_directly(value, axis, dim):
    parts = from_everyone(value, axis)
    return in_order(parts, dim)


def split_up(value, dim, peers):
    before, after = (value.shape[:dim], value.shape[dim + 1 :])
    return jnp.moveaxis(value.reshape(*before, peers, -1, *after), dim, 0)


def summed_on_arrival(value, axis, dim):
    parts = split_up(value, dim, lax.axis_size(axis))
    arrived = lax.all_to_all(parts, axis, split_axis=0, concat_axis=0, tiled=True)
    return arrived.astype(jnp.float32).sum(axis=0)


def bias_table(buckets, time_bias):
    levels = jnp.arange(time_bias.shape[0], dtype=jnp.int32)
    picked = (buckets[:, None] == levels[None, :]).astype(jnp.float32)
    return jnp.dot(picked, time_bias, precision=lax.Precision.HIGHEST)


def weighted_sum(keys_part, values_part, queries, key_bias, allowed, scale_factor):
    scores = jnp.einsum("khd,qhd->hkq", keys_part, queries, preferred_element_type=jnp.float32)
    scores = scores * scale_factor + key_bias.T[:, :, None]
    weights = jnp.where(allowed, jax.nn.silu(scores), 0.0).astype(jnp.bfloat16)
    return jnp.einsum("hkq,khd->qhd", weights, values_part, preferred_element_type=jnp.float32)


def shards(
    events,
    owner_id,
    event_bucket,
    cross_weight,
    cross_bias,
    project_weight,
    cache_keys,
    cache_values,
    cache_length,
    cache_bucket,
    time_bias,
    norm_gain,
):
    row_count, feature_width = events.shape
    head_count = H
    head_width = feature_width // head_count
    owner_count = lax.axis_size("users")
    context_count = lax.axis_size("ctx")
    context_index = lax.axis_index("ctx")
    capacity = max(2, (3 * row_count + 2 * owner_count - 1) // (2 * owner_count))
    slot_count = owner_count * capacity
    cache_rows = cache_keys.shape[1]
    scale_factor = head_width ** (-0.5)
    source = events.astype(jnp.float32)
    cross_full = gather_directly(cross_weight, "users", 0)
    crossing = jnp.dot(events, cross_full, preferred_element_type=jnp.float32)
    crossed = (source * (crossing + cross_bias) + source).astype(jnp.bfloat16)
    owners = owner_id[:, 0]
    positions = jnp.arange(row_count, dtype=jnp.int32)
    earlier = (owners[None, :] == owners[:, None]) & (positions[None, :] < positions[:, None])
    ranking = jnp.sum(earlier.astype(jnp.int32), axis=1)
    slot_of_row = owners * capacity + ranking
    placing = jnp.arange(slot_count, dtype=jnp.int32)[:, None] == slot_of_row[None, :]
    placing_matrix = placing.astype(jnp.bfloat16)
    outgoing = jnp.dot(placing_matrix, crossed, preferred_element_type=jnp.float32).astype(
        jnp.bfloat16
    )
    labels = jnp.sum(jnp.where(placing, event_bucket[None, :] + 1, 0), axis=1).astype(jnp.bfloat16)
    arrived, arrived_labels = (
        lax.all_to_all(
            outgoing.reshape(owner_count, capacity, feature_width),
            "users",
            split_axis=0,
            concat_axis=0,
            tiled=True,
        ),
        lax.all_to_all(
            labels.reshape(owner_count, capacity), "users", split_axis=0, concat_axis=0, tiled=True
        ),
    )
    arrived = arrived.reshape(slot_count, feature_width)
    label_values = arrived_labels.reshape(slot_count).astype(jnp.int32)
    project_full = lax.all_gather(project_weight, "users", axis=0, tiled=True)
    projected = jnp.dot(arrived, project_full, preferred_element_type=jnp.float32)
    activated = jax.nn.silu(projected)
    gate_units = activated[:, :feature_width].astype(jnp.bfloat16)
    new_values = (
        activated[:, feature_width : 2 * feature_width]
        .astype(jnp.bfloat16)
        .reshape(slot_count, head_count, head_width)
    )
    new_queries = activated[:, 2 * feature_width : 3 * feature_width].astype(jnp.bfloat16)
    new_keys = (
        activated[:, 3 * feature_width :]
        .astype(jnp.bfloat16)
        .reshape(slot_count, head_count, head_width)
    )
    slot_index = jnp.arange(slot_count, dtype=jnp.int32)
    key_order = (
        slot_index // capacity * context_count + context_index
    ) * capacity + slot_index % capacity
    key_valid = label_values > 0
    new_bias = bias_table(jnp.maximum(label_values - 1, 0), time_bias)
    cache_key_heads = cache_keys[0].reshape(cache_rows, head_count, head_width)
    cache_value_heads = cache_values[0].reshape(cache_rows, head_count, head_width)
    cache_bias = bias_table(cache_bucket[0], time_bias)
    live_length = cache_length[0] - context_index * cache_rows
    cache_live = jnp.arange(cache_rows, dtype=jnp.int32) < live_length
    block_keys = min(256, cache_rows)
    block_total = cache_rows // block_keys

    def attend_block(query_rows, query_start):
        block_rows = query_rows.shape[0]
        queries = query_rows.reshape(block_rows, head_count, head_width)
        query_index = query_start + jnp.arange(block_rows, dtype=jnp.int32)
        query_context = query_index // slot_count
        query_slot = query_index % slot_count
        query_order = (
            query_slot // capacity * context_count + query_context
        ) * capacity + query_slot % capacity
        allowed = key_valid[None, :, None] & (
            key_order[None, :, None] <= query_order[None, None, :]
        )
        summed = weighted_sum(new_keys, new_values, queries, new_bias, allowed, scale_factor)

        def add_block(block_number, carried):
            offset = block_number * block_keys
            keys_part = lax.dynamic_slice_in_dim(cache_key_heads, offset, block_keys, 0)
            values_part = lax.dynamic_slice_in_dim(cache_value_heads, offset, block_keys, 0)
            bias_part = lax.dynamic_slice_in_dim(cache_bias, offset, block_keys, 0)
            live_part = lax.dynamic_slice_in_dim(cache_live, offset, block_keys, 0)
            return carried + weighted_sum(
                keys_part, values_part, queries, bias_part, live_part[None, :, None], scale_factor
            )

        summed = lax.fori_loop(0, block_total, add_block, summed)
        return summed.reshape(block_rows, feature_width)

    query_piece = lax.all_gather(new_queries, "ctx", axis=0, tiled=True)
    piece_rows = query_piece.shape[0]
    block_count = piece_rows // 512
    stacked = query_piece.reshape(block_count, 512, feature_width)
    block_starts = 512 * jnp.arange(block_count, dtype=jnp.int32)

    def one_block(bundle):
        return attend_block(bundle[0], bundle[1])

    outputs = lax.map(one_block, (stacked, block_starts))
    partials = outputs.reshape(piece_rows, feature_width)
    attended = summed_on_arrival(partials.astype(jnp.bfloat16), "ctx", 0)
    center = jnp.mean(attended, axis=1, keepdims=True)
    spread = jnp.mean(jnp.square(attended - center), axis=1, keepdims=True)
    normed = (attended - center) * lax.rsqrt(spread + norm_epsilon)
    gated = (normed * norm_gain * gate_units.astype(jnp.float32)).astype(jnp.bfloat16)
    returned = lax.all_to_all(
        gated.reshape(owner_count, capacity, feature_width),
        "users",
        split_axis=0,
        concat_axis=0,
        tiled=True,
    )
    result = lax.dot_general(
        placing_matrix,
        returned.reshape(slot_count, feature_width),
        (((0,), (0,)), ((), ())),
        preferred_element_type=jnp.float32,
    )
    return result.astype(jnp.bfloat16)


def solution(mesh):
    return jax.shard_map(
        shards,
        mesh=mesh,
        in_specs=(
            P(("users", "ctx"), None),
            P(("users", "ctx"), None),
            P(("users", "ctx")),
            P("users", None),
            P(),
            P("users", None),
            P("users", "ctx", None),
            P("users", "ctx", None),
            P("users"),
            P("users", "ctx"),
            P(),
            P(),
        ),
        out_specs=P(("users", "ctx"), None),
        check_vma=False,
    )
```

profile of v0, /device:TPU:1, one launch (start us, length us, event | category | flops | bytes accessed | tf_op | source)
XLA Modules:
  0.0 300.3 jit_solution(16034690586346479970)
XLA Ops:
  9.6 15.0 %all-to-all-start.1 = ((bf16[64,16,1024]{2,1,0:T(8,128)(2,1)}), bf16[64,16,1024]{2,1,0:T(8,128)(2,1)S(1)}, u32[]{:S(2)}, u32[]{:S(2)}) async-start(bf16[64,16,1024]{2,1,0:T(8,128)(2,1)} %broadcast_in_dim.96), calls=%async_computation.1 | async-start | bytes 4194304 | tf_op jit(solution)/shard_map/all_to_all | solution.py:12
  24.9 54.3 %all-to-all-done.1 = bf16[64,16,1024]{2,1,0:T(8,128)(2,1)S(1)} async-done(((bf16[64,16,1024]{2,1,0:T(8,128)(2,1)}), bf16[64,16,1024]{2,1,0:T(8,128)(2,1)S(1)}, u32[]{:S(2)}, u32[]{:S(2)}) %all-to-all-start.1) | async-done | bytes 2097184 | tf_op jit(solution)/shard_map/all_to_all | solution.py:12
  80.0 21.7 %all_to_all.26 = bf16[64,2,1024]{2,1,0:T(2,128)(2,1)S(1)} all-to-all(bf16[64,2,1024]{2,1,0:T(2,128)(2,1)S(1)} %reshape.197), channel_id=1, replica_groups=mesh['users'=64,'ctx'=8] {'users'}, dimensions={0} | all-to-all | bytes 524288 | tf_op jit(solution)/shard_map/all_to_all | solution.py:90
  101.8 14.6 %all-gather.3.cloned.1.call-done = bf16[1024,4096]{1,0:T(8,128)(2,1)} async-done(((bf16[16,4096]{1,0:T(8,128)(2,1)}), bf16[1024,4096]{1,0:T(8,128)(2,1)}) %all-gather.3.cloned.1.call-update) | async-done | bytes 8388624 | tf_op jit(solution)/shard_map/all_gather | solution.py:103
  116.5 4.7 %multiply_convert_fusion = bf16[128,4096]{1,0:T(8,128)(2,1)S(1)} fusion(bf16[128,1024]{1,0:T(8,128)(2,1)S(1)} %reshape.198, bf16[1024,4096]{1,0:T(8,128)(2,1)} %all-gather.3.cloned.1.call-done), kind=kOutput, calls=%fused_computation.63 | convolution fusion | flops 1076363264 | bytes 9699328 | tf_op jit(solution)/shard_map/dot_general | solution.py:104
  124.0 7.0 %all-to-all-start = ((bf16[64,1,2]{2,1,0:T(2,128)(2,1)}), bf16[64,1,2]{2,1,0:T(2,128)(2,1)S(1)}, u32[]{:S(2)}, u32[]{:S(2)}) async-start(bf16[64,1,2]{2,1,0:T(2,128)(2,1)} %convert_element_type.88), calls=%async_computation | async-start | bytes 65536 | tf_op jit(solution)/shard_map/all_to_all | solution.py:97
  131.6 2.9 copy.43
  137.3 3.9 %copy.42 = bf16[1,1024,1024]{1,2,0:T(8,128)(2,1)} copy(bf16[1,1024,1024]{2,1,0:T(8,128)(2,1)} %param.23) | data formatting | bytes 4194304 | tf_op args[7]
  142.2 18.1 %all-gather.5.cloned.1.call-done = bf16[1024,1024]{1,0:T(8,128)(2,1)} async-done(((bf16[128,1024]{1,0:T(8,128)(2,1)}), bf16[1024,1024]{1,0:T(8,128)(2,1)}) %all-gather.5.cloned.1.call-update) | async-done | bytes 2097168 | tf_op jit(solution)/shard_map/all_gather | solution.py:159
  160.3 50.7 %while.38 = (s32[]{:T(128)}, bf16[2,512,1024]{2,1,0:T(8,128)(2,1)}, pred[128]{0:T(512)(128)(4,1)S(1)}, s32[2]{0:T(128)S(1)}, bf16[2,512,1024]{2,1,0:T(8,128)(2,1...) while((s32[]{:T(128)}, bf16[2,512,1024]{2,1,0:T(8,128)(2,1)}, ...), condition=%wide.region_5.6_spmd.clone, body=%wide.region_2.5_spmd.clone.sunk | while | flops 818569728 | bytes 27956100 | solution.py:168
  163.6 2.5 convolution_bitcast_fusion.2
  169.3 14.6 %while.39 = (s32[]{:T(128)}, f32[512,8,128]{0,2,1:T(8,128)S(1)}, bf16[1024,8,128]{0,2,1:T(8,128)(2,1)}, pred[1024]{0:T(1024)(128)(4,1)S(1)}, bf16[1024,8,128]{2,...) while((s32[]{:T(128)}, f32[512,8,128]{0,2,1:T(8,128)S(1)}, ...), condition=%wide.region_4.4_spmd, body=%wide.region_3.3_spmd.sunk | while | flops 545783808 | bytes 6317987 | solution.py:156
  169.4 3.5 %bitcast_add_fusion.2 = f32[512,8,128]{0,2,1:T(8,128)S(1)} fusion(f32[512,8,128]{0,2,1:T(8,128)S(1)} %get-tuple-element.659, bf16[512,8,128]{2,0,1:T(8,128)(2,1)} %get-tuple-element.674, f32[8,256]{1,0:T(8,128)S(1)} %dynamic-slice_bitcast_fusion.2, pred[256]{0:T(512)(128)(4,1)S(1)} %dynamic_slice.64, bf16[1024,8,128]{2,0,1:T(8,128)(2,1)} %get-tuple-element.673, ...), kind=kOutput, calls=%fused_computation.3.clone.1 | convolution fusion | flops 545783808 | bytes 6300928 | tf_op jit(solution)/shard_map/while/body/eval_jaxpr/while/body/eval_jaxpr/hkq,khd->qhd/dot_general | solution.py:47
  173.1 3.5 %bitcast_add_fusion.2 = f32[512,8,128]{0,2,1:T(8,128)S(1)} fusion(f32[512,8,128]{0,2,1:T(8,128)S(1)} %get-tuple-element.659, bf16[512,8,128]{2,0,1:T(8,128)(2,1)} %get-tuple-element.674, f32[8,256]{1,0:T(8,128)S(1)} %dynamic-slice_bitcast_fusion.2, pred[256]{0:T(512)(128)(4,1)S(1)} %dynamic_slice.64, bf16[1024,8,128]{2,0,1:T(8,128)(2,1)} %get-tuple-element.673, ...), kind=kOutput, calls=%fused_computation.3.clone.1 | convolution fusion | flops 545783808 | bytes 6300928 | tf_op jit(solution)/shard_map/while/body/eval_jaxpr/while/body/eval_jaxpr/hkq,khd->qhd/dot_general | solution.py:47
  176.7 3.5 %bitcast_add_fusion.2 = f32[512,8,128]{0,2,1:T(8,128)S(1)} fusion(f32[512,8,128]{0,2,1:T(8,128)S(1)} %get-tuple-element.659, bf16[512,8,128]{2,0,1:T(8,128)(2,1)} %get-tuple-element.674, f32[8,256]{1,0:T(8,128)S(1)} %dynamic-slice_bitcast_fusion.2, pred[256]{0:T(512)(128)(4,1)S(1)} %dynamic_slice.64, bf16[1024,8,128]{2,0,1:T(8,128)(2,1)} %get-tuple-element.673, ...), kind=kOutput, calls=%fused_computation.3.clone.1 | convolution fusion | flops 545783808 | bytes 6300928 | tf_op jit(solution)/shard_map/while/body/eval_jaxpr/while/body/eval_jaxpr/hkq,khd->qhd/dot_general | solution.py:47
  180.4 3.5 %bitcast_add_fusion.2 = f32[512,8,128]{0,2,1:T(8,128)S(1)} fusion(f32[512,8,128]{0,2,1:T(8,128)S(1)} %get-tuple-element.659, bf16[512,8,128]{2,0,1:T(8,128)(2,1)} %get-tuple-element.674, f32[8,256]{1,0:T(8,128)S(1)} %dynamic-slice_bitcast_fusion.2, pred[256]{0:T(512)(128)(4,1)S(1)} %dynamic_slice.64, bf16[1024,8,128]{2,0,1:T(8,128)(2,1)} %get-tuple-element.673, ...), kind=kOutput, calls=%fused_computation.3.clone.1 | convolution fusion | flops 545783808 | bytes 6300928 | tf_op jit(solution)/shard_map/while/body/eval_jaxpr/while/body/eval_jaxpr/hkq,khd->qhd/dot_general | solution.py:47
  188.9 2.5 convolution_bitcast_fusion.2
  194.7 14.6 %while.39 = (s32[]{:T(128)}, f32[512,8,128]{0,2,1:T(8,128)S(1)}, bf16[1024,8,128]{0,2,1:T(8,128)(2,1)}, pred[1024]{0:T(1024)(128)(4,1)S(1)}, bf16[1024,8,128]{2,...) while((s32[]{:T(128)}, f32[512,8,128]{0,2,1:T(8,128)S(1)}, ...), condition=%wide.region_4.4_spmd, body=%wide.region_3.3_spmd.sunk | while | flops 545783808 | bytes 6317987 | solution.py:156
  194.7 3.5 %bitcast_add_fusion.2 = f32[512,8,128]{0,2,1:T(8,128)S(1)} fusion(f32[512,8,128]{0,2,1:T(8,128)S(1)} %get-tuple-element.659, bf16[512,8,128]{2,0,1:T(8,128)(2,1)} %get-tuple-element.674, f32[8,256]{1,0:T(8,128)S(1)} %dynamic-slice_bitcast_fusion.2, pred[256]{0:T(512)(128)(4,1)S(1)} %dynamic_slice.64, bf16[1024,8,128]{2,0,1:T(8,128)(2,1)} %get-tuple-element.673, ...), kind=kOutput, calls=%fused_computation.3.clone.1 | convolution fusion | flops 545783808 | bytes 6300928 | tf_op jit(solution)/shard_map/while/body/eval_jaxpr/while/body/eval_jaxpr/hkq,khd->qhd/dot_general | solution.py:47
  198.4 3.5 %bitcast_add_fusion.2 = f32[512,8,128]{0,2,1:T(8,128)S(1)} fusion(f32[512,8,128]{0,2,1:T(8,128)S(1)} %get-tuple-element.659, bf16[512,8,128]{2,0,1:T(8,128)(2,1)} %get-tuple-element.674, f32[8,256]{1,0:T(8,128)S(1)} %dynamic-slice_bitcast_fusion.2, pred[256]{0:T(512)(128)(4,1)S(1)} %dynamic_slice.64, bf16[1024,8,128]{2,0,1:T(8,128)(2,1)} %get-tuple-element.673, ...), kind=kOutput, calls=%fused_computation.3.clone.1 | convolution fusion | flops 545783808 | bytes 6300928 | tf_op jit(solution)/shard_map/while/body/eval_jaxpr/while/body/eval_jaxpr/hkq,khd->qhd/dot_general | solution.py:47
  202.1 3.5 %bitcast_add_fusion.2 = f32[512,8,128]{0,2,1:T(8,128)S(1)} fusion(f32[512,8,128]{0,2,1:T(8,128)S(1)} %get-tuple-element.659, bf16[512,8,128]{2,0,1:T(8,128)(2,1)} %get-tuple-element.674, f32[8,256]{1,0:T(8,128)S(1)} %dynamic-slice_bitcast_fusion.2, pred[256]{0:T(512)(128)(4,1)S(1)} %dynamic_slice.64, bf16[1024,8,128]{2,0,1:T(8,128)(2,1)} %get-tuple-element.673, ...), kind=kOutput, calls=%fused_computation.3.clone.1 | convolution fusion | flops 545783808 | bytes 6300928 | tf_op jit(solution)/shard_map/while/body/eval_jaxpr/while/body/eval_jaxpr/hkq,khd->qhd/dot_general | solution.py:47
  205.7 3.5 %bitcast_add_fusion.2 = f32[512,8,128]{0,2,1:T(8,128)S(1)} fusion(f32[512,8,128]{0,2,1:T(8,128)S(1)} %get-tuple-element.659, bf16[512,8,128]{2,0,1:T(8,128)(2,1)} %get-tuple-element.674, f32[8,256]{1,0:T(8,128)S(1)} %dynamic-slice_bitcast_fusion.2, pred[256]{0:T(512)(128)(4,1)S(1)} %dynamic_slice.64, bf16[1024,8,128]{2,0,1:T(8,128)(2,1)} %get-tuple-element.673, ...), kind=kOutput, calls=%fused_computation.3.clone.1 | convolution fusion | flops 545783808 | bytes 6300928 | tf_op jit(solution)/shard_map/while/body/eval_jaxpr/while/body/eval_jaxpr/hkq,khd->qhd/dot_general | solution.py:47
  211.0 49.5 %all_to_all.27 = bf16[8,128,1024]{2,1,0:T(8,128)(2,1)S(1)} all-to-all(bf16[8,128,1024]{2,1,0:T(8,128)(2,1)} %bitcast.87), channel_id=1, replica_groups=mesh['users'=64,'ctx'=8] {'ctx'}, dimensions={0} | all-to-all | bytes 4194304 | tf_op jit(solution)/shard_map/all_to_all | solution.py:33
  262.5 30.0 %all_to_all.28 = bf16[64,2,1024]{2,1,0:T(2,128)(2,1)S(1)} all-to-all(bf16[64,2,1024]{2,1,0:T(2,128)(2,1)S(1)} %reshape.202), channel_id=1, replica_groups=mesh['users'=64,'ctx'=8] {'users'}, dimensions={0} | all-to-all | bytes 524288 | tf_op jit(solution)/shard_map/all_to_all | solution.py:175
  (100 shorter events, 30.7 us)
Async XLA Ops:
  6.5 127.9 %copy-start = (f32[32,8]{0,1:T(8,128)S(1)}, f32[32,8]{0,1:T(8,128)}, u32[]{:S(2)}) copy-start(f32[32,8]{0,1:T(8,128)} %param.26) | copy-start | bytes 3076
  6.5 109.9 %all-gather.3.cloned.1.call-start = ((), (), s32[]{:S(2)}) async-start(), calls=%async_computation.5 | async-start | bytes 8519680 | tf_op jit(solution)/shard_map/all_gather | solution.py:103
  9.6 15.0 %copy-start.10 = (s32[64,1]{0,1:T(1,128)S(1)}, s32[64,1]{0,1:T(1,128)}, u32[]{:S(2)}) copy-start(s32[64,1]{0,1:T(1,128)} %param.17) | copy-start | bytes 772
  9.6 69.6 %copy-start.4 = (bf16[64,1024]{1,0:T(8,128)(2,1)S(1)}, bf16[64,1024]{1,0:T(8,128)(2,1)}, u32[]{:S(2)}) copy-start(bf16[64,1024]{1,0:T(8,128)(2,1)} %param.16) | copy-start | bytes 393220
  9.6 69.6 %copy-start.5 = (f32[1024]{0:T(1024)S(1)}, f32[1024]{0:T(1024)}, u32[]{:S(2)}) copy-start(f32[1024]{0:T(1024)} %param.20) | copy-start | bytes 12292
  9.6 69.6 %all-to-all-start.1 = ((bf16[64,16,1024]{2,1,0:T(8,128)(2,1)}), bf16[64,16,1024]{2,1,0:T(8,128)(2,1)S(1)}, u32[]{:S(2)}, u32[]{:S(2)}) async-start(bf16[64,16,1024]{2,1,0:T(8,128)(2,1)} %broadcast_in_dim.96), calls=%async_computation.1 | async-start | bytes 4194304 | tf_op jit(solution)/shard_map/all_to_all | solution.py:12
  24.6 135.7 %all-gather.5.cloned.1.call-start = ((), (), s32[]{:S(2)}) async-start(), calls=%async_computation.6 | async-start | bytes 2359296 | tf_op jit(solution)/shard_map/all_gather | solution.py:159
  24.9 98.2 %copy-start.7 = (s32[64]{0:T(128)}, s32[64]{0:T(128)S(1)}, u32[]{:S(2)}) copy-start(s32[64]{0:T(128)S(1)} %multiply_add_fusion) | copy-start | bytes 772
  101.8 21.2 %copy-start.11 = (s32[64]{0:T(128)S(1)}, s32[64]{0:T(128)}, u32[]{:S(2)}) copy-start(s32[64]{0:T(128)} %param.18) | copy-start | bytes 772
  121.2 1.0 copy-start.1
  124.0 17.3 %all-to-all-start = ((bf16[64,1,2]{2,1,0:T(2,128)(2,1)}), bf16[64,1,2]{2,1,0:T(2,128)(2,1)S(1)}, u32[]{:S(2)}, u32[]{:S(2)}) async-start(bf16[64,1,2]{2,1,0:T(2,128)(2,1)} %convert_element_type.88), calls=%async_computation | async-start | bytes 65536 | tf_op jit(solution)/shard_map/all_to_all | solution.py:97
  131.6 2.9 copy-start.9
  160.3 3.3 %copy-start.2 = (bf16[128,8,128]{2,0,1:T(8,128)(2,1)}, bf16[128,8,128]{2,0,1:T(8,128)(2,1)S(1)}, u32[]{:S(2)}) copy-start(bf16[128,8,128]{2,0,1:T(8,128)(2,1)S(1)} %get-tuple-element.723) | copy-start | bytes 786436 | tf_op jit(solution)/shard_map/while
  184.5 1.1 copy-start.3
  185.6 3.3 %copy-start.2 = (bf16[128,8,128]{2,0,1:T(8,128)(2,1)}, bf16[128,8,128]{2,0,1:T(8,128)(2,1)S(1)}, u32[]{:S(2)}) copy-start(bf16[128,8,128]{2,0,1:T(8,128)(2,1)S(1)} %get-tuple-element.723) | copy-start | bytes 786436 | tf_op jit(solution)/shard_map/while
  209.9 1.1 copy-start.3
  260.5 0.7 copy-start.6
  261.0 31.6 %copy-start.8 = (s32[64]{0:T(128)S(1)}, s32[64]{0:T(128)}, u32[]{:S(2)}) copy-start(s32[64]{0:T(128)} %copy-done.7) | copy-start | bytes 772
Sparse Core Ops, SparseCore 0:
  10.7 105.7 all-gather.2
  123.1 37.1 all-gather.4
where the time goes:
time: 301 us; the launch traced here: 300 us
  blocking collectives  101 us (34%)
  waiting for transfers between devices  87.8 us (29%)
  matrix products  40.1 us (13%)
  local copies, waits for them, and re-layouts  30.5 us (10%)
  starting transfers between devices  22 us (7%)
  between operations  14.3 us (5%)
  other arithmetic  4.04 us (1%)
    all_to_all x1, waiting for transfers between devices, from_everyone(): return lax.all_to_all(copies, axis, split_axis=0, concat_axis=0, tiled=True)  54.3 us
    all_to_all x1, blocking collectives, summed_on_arrival(): lax.all_to_all(parts, axis, split_axis=0, concat_axis=0, tiled=True)  49.5 us
    dot_general x10, matrix products, weighted_sum(): jnp.einsum('hkq,khd->qhd', weights, values_part, preferred_element_type=j...  33.2 us
    all_to_all x1, blocking collectives, shards(): lax.all_to_all(gated.reshape(owner_count, capacity, feature_width), 'user...  30 us
    all_to_all x1, blocking collectives, shards(): lax.all_to_all(outgoing.reshape(owner_count, capacity, feature_width), 'u...  21.7 us
    all_gather x1, waiting for transfers between devices, shards(): query_piece = lax.all_gather(new_queries, 'ctx', axis=0, tiled=True)  18.1 us
    all_to_all x1, starting transfers between devices, from_everyone(): return lax.all_to_all(copies, axis, split_axis=0, concat_axis=0, tiled=True)  15 us
    all_gather x1, waiting for transfers between devices, shards(): project_full = lax.all_gather(project_weight, 'users', axis=0, tiled=True)  14.6 us
  transfers between devices with their start and end apart: 4, of which 3 were waited for; matrix products, arithmetic and copies ran while one was open for 5% of the time, Pallas kernels for 0%

commit v1 on v0

--- a/solution.py
+++ b/solution.py
@@ -156,7 +156,9 @@
         summed = lax.fori_loop(0, block_total, add_block, summed)
         return summed.reshape(block_rows, feature_width)
 
-    query_piece = lax.all_gather(new_queries, "ctx", axis=0, tiled=True)
+    query_piece = jnp.concatenate(
+        lax.all_to_all(jnp.stack([new_queries] * lax.axis_size("ctx")), "ctx", 0, 0), axis=0
+    )
     piece_rows = query_piece.shape[0]
     block_count = piece_rows // 512
     stacked = query_piece.reshape(block_count, 512, feature_width)

time: 301 us -> 317 us (1.053)
  waiting for transfers between devices: 87.8 us -> 115 us
  blocking collectives: 101 us -> 75.7 us
  starting transfers between devices: 22 us -> 33.6 us
    all_to_all x0 -> x2, waiting for transfers between devices: none -> 51.6 us  [the longest x1 37.1 us: shards(): lax.all_to_all(jnp.stack([new_queries] * lax.axis_size('ctx')), 'ctx', 0, 0)]
    all_to_all x1 -> x0, blocking collectives: 21.7 us -> none  [shards(): lax.all_to_all(outgoing.reshape(owner_count, capacity, feature_width), 'u...]
    all_gather x1 -> x0, waiting for transfers between devices: 18.1 us -> none  [shards(): query_piece = lax.all_gather(new_queries, 'ctx', axis=0, tiled=True)]
    all_to_all x0 -> x2, starting transfers between devices: none -> 13.8 us  [the longest x1 7.02 us: shards(): lax.all_to_all(outgoing.reshape(owner_count, capacity, feature_width), 'u...]
    all_to_all x1, blocking collectives: 30 us -> 22.9 us  [shards(): lax.all_to_all(gated.reshape(owner_count, capacity, feature_width), 'user...]
    all_gather x1, waiting for transfers between devices: 14.6 us -> 8.63 us  [shards(): project_full = lax.all_gather(project_weight, 'users', axis=0, tiled=True)]
    all_to_all x1, blocking collectives: 49.5 us -> 52.8 us  [summed_on_arrival(): lax.all_to_all(parts, axis, split_axis=0, concat_axis=0, tiled=True)]
  transfers between devices with their start and end apart: 4 -> 5, of which waited for: 3 -> 4; matrix products, arithmetic and copies ran while one was open for 5% -> 6% of each run, Pallas kernels for 0% -> 0%
where the time goes in v1:
time: 317 us; the launch traced here: 316 us
  waiting for transfers between devices  115 us (36%)
  blocking collectives  75.7 us (24%)
  matrix products  40.1 us (13%)
  starting transfers between devices  33.6 us (11%)
  local copies, waits for them, and re-layouts  32.2 us (10%)
  between operations  14.2 us (4%)
  other arithmetic  4.1 us (1%)
    all_to_all x1, waiting for transfers between devices, from_everyone(): return lax.all_to_all(copies, axis, split_axis=0, concat_axis=0, tiled=True)  54.4 us
    all_to_all x1, blocking collectives, summed_on_arrival(): lax.all_to_all(parts, axis, split_axis=0, concat_axis=0, tiled=True)  52.8 us
    all_to_all x1, waiting for transfers between devices, shards(): lax.all_to_all(jnp.stack([new_queries] * lax.axis_size('ctx')), 'ctx', 0, 0)  37.1 us
    dot_general x10, matrix products, weighted_sum(): jnp.einsum('hkq,khd->qhd', weights, values_part, preferred_element_type=j...  33.2 us
    all_to_all x1, blocking collectives, shards(): lax.all_to_all(gated.reshape(owner_count, capacity, feature_width), 'user...  22.9 us
    all_to_all x1, starting transfers between devices, from_everyone(): return lax.all_to_all(copies, axis, split_axis=0, concat_axis=0, tiled=True)  15 us
    all_to_all x1, waiting for transfers between devices, shards(): lax.all_to_all(outgoing.reshape(owner_count, capacity, feature_width), 'u...  14.4 us
    unnamed x25, local copies, waits for them, and re-layouts  10.4 us
  transfers between devices with their start and end apart: 5, of which 4 were waited for; matrix products, arithmetic and copies ran while one was open for 6% of the time, Pallas kernels for 0%

profile of v1, /device:TPU:1, one launch (start us, length us, event | category | flops | bytes accessed | tf_op | source)
XLA Modules:
  0.0 315.7 jit_solution(11716987560286439453)
XLA Ops:
  9.6 15.0 %all-to-all-start.1 = ((bf16[64,16,1024]{2,1,0:T(8,128)(2,1)}), bf16[64,16,1024]{2,1,0:T(8,128)(2,1)S(1)}, u32[]{:S(2)}, u32[]{:S(2)}) async-start(bf16[64,16,1024]{2,1,0:T(8,128)(2,1)} %broadcast_in_dim.96), calls=%async_computation.1 | async-start | bytes 4194304 | tf_op jit(solution)/shard_map/all_to_all | solution.py:12
  24.8 54.4 %all-to-all-done.1 = bf16[64,16,1024]{2,1,0:T(8,128)(2,1)S(1)} async-done(((bf16[64,16,1024]{2,1,0:T(8,128)(2,1)}), bf16[64,16,1024]{2,1,0:T(8,128)(2,1)S(1)}, u32[]{:S(2)}, u32[]{:S(2)}) %all-to-all-start.1) | async-done | bytes 2097184 | tf_op jit(solution)/shard_map/all_to_all | solution.py:12
  80.7 7.0 %all-to-all-start.2 = ((bf16[64,2,1024]{2,1,0:T(2,128)(2,1)}), bf16[64,2,1024]{2,1,0:T(2,128)(2,1)S(1)}, u32[]{:S(2)}, u32[]{:S(2)}) async-start(bf16[64,2,1024]{2,1,0:T(2,128)(2,1)} %reshape.196), calls=%async_computation.2 | async-start | bytes 524288 | tf_op jit(solution)/shard_map/all_to_all | solution.py:90
  88.7 14.4 %all-to-all-done.2 = bf16[64,2,1024]{2,1,0:T(2,128)(2,1)S(1)} async-done(((bf16[64,2,1024]{2,1,0:T(2,128)(2,1)}), bf16[64,2,1024]{2,1,0:T(2,128)(2,1)S(1)}, u32[]{:S(2)}, u32[]{:S(2)}) %all-to-all-start.2) | async-done | bytes 262176 | tf_op jit(solution)/shard_map/all_to_all | solution.py:90
  103.1 4.9 %all-to-all-start = ((bf16[64,1,2]{2,1,0:T(2,128)(2,1)}), bf16[64,1,2]{2,1,0:T(2,128)(2,1)S(1)}, u32[]{:S(2)}, u32[]{:S(2)}) async-start(bf16[64,1,2]{2,1,0:T(2,128)(2,1)} %convert_element_type.88), calls=%async_computation | async-start | bytes 65536 | tf_op jit(solution)/shard_map/all_to_all | solution.py:97
  108.1 8.6 %all-gather.2.cloned.1.call-done = bf16[1024,4096]{1,0:T(8,128)(2,1)} async-done(((bf16[16,4096]{1,0:T(8,128)(2,1)}), bf16[1024,4096]{1,0:T(8,128)(2,1)}) %all-gather.2.cloned.1.call-update) | async-done | bytes 8388624 | tf_op jit(solution)/shard_map/all_gather | solution.py:103
  116.7 4.7 %multiply_convert_fusion = bf16[128,4096]{1,0:T(8,128)(2,1)S(1)} fusion(bf16[128,1024]{1,0:T(8,128)(2,1)S(1)} %reshape.197, bf16[1024,4096]{1,0:T(8,128)(2,1)} %all-gather.2.cloned.1.call-done), kind=kOutput, calls=%fused_computation.63 | convolution fusion | flops 1076363264 | bytes 9699328 | tf_op jit(solution)/shard_map/dot_general | solution.py:104
  124.2 6.7 %all-to-all-start.3 = ((bf16[8,128,1024]{2,1,0:T(8,128)(2,1)}), bf16[8,128,1024]{2,1,0:T(8,128)(2,1)}, u32[]{:S(2)}, u32[]{:S(2)}) async-start(bf16[8,128,1024]{2,1,0:T(8,128)(2,1)} %stack.2), calls=%async_computation.3 | async-start | bytes 4194304 | tf_op jit(solution)/shard_map/all_to_all | solution.py:160
  131.6 2.9 copy.52
  136.8 3.9 %copy.51 = bf16[1,1024,1024]{1,2,0:T(8,128)(2,1)} copy(bf16[1,1024,1024]{2,1,0:T(8,128)(2,1)} %param.23) | data formatting | bytes 4194304 | tf_op args[7]
  142.2 37.1 %all-to-all-done.3 = bf16[8,128,1024]{2,1,0:T(8,128)(2,1)} async-done(((bf16[8,128,1024]{2,1,0:T(8,128)(2,1)}), bf16[8,128,1024]{2,1,0:T(8,128)(2,1)}, u32[]{:S(2)}, u32[]{:S(2)}) %all-to-all-start.3) | async-done | bytes 2097184 | tf_op jit(solution)/shard_map/all_to_all | solution.py:160
  179.3 50.8 %while.38 = (s32[]{:T(128)}, bf16[2,512,1024]{2,1,0:T(8,128)(2,1)}, pred[128]{0:T(512)(128)(4,1)S(1)}, s32[2]{0:T(128)S(1)}, bf16[2,512,1024]{2,1,0:T(8,128)(2,1...) while((s32[]{:T(128)}, bf16[2,512,1024]{2,1,0:T(8,128)(2,1)}, ...), condition=%wide.region_5.6_spmd.clone, body=%wide.region_2.5_spmd.clone.sunk | while | flops 818569728 | bytes 27956100 | solution.py:170
  188.4 14.6 %while.39 = (s32[]{:T(128)}, f32[512,8,128]{0,2,1:T(8,128)S(1)}, bf16[1024,8,128]{0,2,1:T(8,128)(2,1)}, pred[1024]{0:T(1024)(128)(4,1)S(1)}, bf16[1024,8,128]{2,...) while((s32[]{:T(128)}, f32[512,8,128]{0,2,1:T(8,128)S(1)}, ...), condition=%wide.region_4.4_spmd, body=%wide.region_3.3_spmd.sunk | while | flops 545783808 | bytes 6317987 | solution.py:156
  188.5 3.5 %bitcast_add_fusion.2 = f32[512,8,128]{0,2,1:T(8,128)S(1)} fusion(f32[512,8,128]{0,2,1:T(8,128)S(1)} %get-tuple-element.679, bf16[512,8,128]{2,0,1:T(8,128)(2,1)} %get-tuple-element.694, f32[8,256]{1,0:T(8,128)S(1)} %dynamic-slice_bitcast_fusion.2, pred[256]{0:T(512)(128)(4,1)S(1)} %dynamic_slice.64, bf16[1024,8,128]{2,0,1:T(8,128)(2,1)} %get-tuple-element.693, ...), kind=kOutput, calls=%fused_computation.3.clone.1 | convolution fusion | flops 545783808 | bytes 6300928 | tf_op jit(solution)/shard_map/while/body/eval_jaxpr/while/body/eval_jaxpr/hkq,khd->qhd/dot_general | solution.py:47
  192.2 3.5 %bitcast_add_fusion.2 = f32[512,8,128]{0,2,1:T(8,128)S(1)} fusion(f32[512,8,128]{0,2,1:T(8,128)S(1)} %get-tuple-element.679, bf16[512,8,128]{2,0,1:T(8,128)(2,1)} %get-tuple-element.694, f32[8,256]{1,0:T(8,128)S(1)} %dynamic-slice_bitcast_fusion.2, pred[256]{0:T(512)(128)(4,1)S(1)} %dynamic_slice.64, bf16[1024,8,128]{2,0,1:T(8,128)(2,1)} %get-tuple-element.693, ...), kind=kOutput, calls=%fused_computation.3.clone.1 | convolution fusion | flops 545783808 | bytes 6300928 | tf_op jit(solution)/shard_map/while/body/eval_jaxpr/while/body/eval_jaxpr/hkq,khd->qhd/dot_general | solution.py:47
  195.8 3.5 %bitcast_add_fusion.2 = f32[512,8,128]{0,2,1:T(8,128)S(1)} fusion(f32[512,8,128]{0,2,1:T(8,128)S(1)} %get-tuple-element.679, bf16[512,8,128]{2,0,1:T(8,128)(2,1)} %get-tuple-element.694, f32[8,256]{1,0:T(8,128)S(1)} %dynamic-slice_bitcast_fusion.2, pred[256]{0:T(512)(128)(4,1)S(1)} %dynamic_slice.64, bf16[1024,8,128]{2,0,1:T(8,128)(2,1)} %get-tuple-element.693, ...), kind=kOutput, calls=%fused_computation.3.clone.1 | convolution fusion | flops 545783808 | bytes 6300928 | tf_op jit(solution)/shard_map/while/body/eval_jaxpr/while/body/eval_jaxpr/hkq,khd->qhd/dot_general | solution.py:47
  199.5 3.5 %bitcast_add_fusion.2 = f32[512,8,128]{0,2,1:T(8,128)S(1)} fusion(f32[512,8,128]{0,2,1:T(8,128)S(1)} %get-tuple-element.679, bf16[512,8,128]{2,0,1:T(8,128)(2,1)} %get-tuple-element.694, f32[8,256]{1,0:T(8,128)S(1)} %dynamic-slice_bitcast_fusion.2, pred[256]{0:T(512)(128)(4,1)S(1)} %dynamic_slice.64, bf16[1024,8,128]{2,0,1:T(8,128)(2,1)} %get-tuple-element.693, ...), kind=kOutput, calls=%fused_computation.3.clone.1 | convolution fusion | flops 545783808 | bytes 6300928 | tf_op jit(solution)/shard_map/while/body/eval_jaxpr/while/body/eval_jaxpr/hkq,khd->qhd/dot_general | solution.py:47
  213.9 14.6 %while.39 = (s32[]{:T(128)}, f32[512,8,128]{0,2,1:T(8,128)S(1)}, bf16[1024,8,128]{0,2,1:T(8,128)(2,1)}, pred[1024]{0:T(1024)(128)(4,1)S(1)}, bf16[1024,8,128]{2,...) while((s32[]{:T(128)}, f32[512,8,128]{0,2,1:T(8,128)S(1)}, ...), condition=%wide.region_4.4_spmd, body=%wide.region_3.3_spmd.sunk | while | flops 545783808 | bytes 6317987 | solution.py:156
  213.9 3.5 %bitcast_add_fusion.2 = f32[512,8,128]{0,2,1:T(8,128)S(1)} fusion(f32[512,8,128]{0,2,1:T(8,128)S(1)} %get-tuple-element.679, bf16[512,8,128]{2,0,1:T(8,128)(2,1)} %get-tuple-element.694, f32[8,256]{1,0:T(8,128)S(1)} %dynamic-slice_bitcast_fusion.2, pred[256]{0:T(512)(128)(4,1)S(1)} %dynamic_slice.64, bf16[1024,8,128]{2,0,1:T(8,128)(2,1)} %get-tuple-element.693, ...), kind=kOutput, calls=%fused_computation.3.clone.1 | convolution fusion | flops 545783808 | bytes 6300928 | tf_op jit(solution)/shard_map/while/body/eval_jaxpr/while/body/eval_jaxpr/hkq,khd->qhd/dot_general | solution.py:47
  217.6 3.5 %bitcast_add_fusion.2 = f32[512,8,128]{0,2,1:T(8,128)S(1)} fusion(f32[512,8,128]{0,2,1:T(8,128)S(1)} %get-tuple-element.679, bf16[512,8,128]{2,0,1:T(8,128)(2,1)} %get-tuple-element.694, f32[8,256]{1,0:T(8,128)S(1)} %dynamic-slice_bitcast_fusion.2, pred[256]{0:T(512)(128)(4,1)S(1)} %dynamic_slice.64, bf16[1024,8,128]{2,0,1:T(8,128)(2,1)} %get-tuple-element.693, ...), kind=kOutput, calls=%fused_computation.3.clone.1 | convolution fusion | flops 545783808 | bytes 6300928 | tf_op jit(solution)/shard_map/while/body/eval_jaxpr/while/body/eval_jaxpr/hkq,khd->qhd/dot_general | solution.py:47
  221.2 3.5 %bitcast_add_fusion.2 = f32[512,8,128]{0,2,1:T(8,128)S(1)} fusion(f32[512,8,128]{0,2,1:T(8,128)S(1)} %get-tuple-element.679, bf16[512,8,128]{2,0,1:T(8,128)(2,1)} %get-tuple-element.694, f32[8,256]{1,0:T(8,128)S(1)} %dynamic-slice_bitcast_fusion.2, pred[256]{0:T(512)(128)(4,1)S(1)} %dynamic_slice.64, bf16[1024,8,128]{2,0,1:T(8,128)(2,1)} %get-tuple-element.693, ...), kind=kOutput, calls=%fused_computation.3.clone.1 | convolution fusion | flops 545783808 | bytes 6300928 | tf_op jit(solution)/shard_map/while/body/eval_jaxpr/while/body/eval_jaxpr/hkq,khd->qhd/dot_general | solution.py:47
  224.9 3.5 %bitcast_add_fusion.2 = f32[512,8,128]{0,2,1:T(8,128)S(1)} fusion(f32[512,8,128]{0,2,1:T(8,128)S(1)} %get-tuple-element.679, bf16[512,8,128]{2,0,1:T(8,128)(2,1)} %get-tuple-element.694, f32[8,256]{1,0:T(8,128)S(1)} %dynamic-slice_bitcast_fusion.2, pred[256]{0:T(512)(128)(4,1)S(1)} %dynamic_slice.64, bf16[1024,8,128]{2,0,1:T(8,128)(2,1)} %get-tuple-element.693, ...), kind=kOutput, calls=%fused_computation.3.clone.1 | convolution fusion | flops 545783808 | bytes 6300928 | tf_op jit(solution)/shard_map/while/body/eval_jaxpr/while/body/eval_jaxpr/hkq,khd->qhd/dot_general | solution.py:47
  230.1 52.8 %all_to_all.31 = bf16[8,128,1024]{2,1,0:T(8,128)(2,1)S(1)} all-to-all(bf16[8,128,1024]{2,1,0:T(8,128)(2,1)} %bitcast.86), channel_id=1, replica_groups=mesh['users'=64,'ctx'=8] {'ctx'}, dimensions={0} | all-to-all | bytes 4194304 | tf_op jit(solution)/shard_map/all_to_all | solution.py:33
  284.9 22.9 %all_to_all.32 = bf16[64,2,1024]{2,1,0:T(2,128)(2,1)S(1)} all-to-all(bf16[64,2,1024]{2,1,0:T(2,128)(2,1)S(1)} %reshape.200), channel_id=1, replica_groups=mesh['users'=64,'ctx'=8] {'users'}, dimensions={0} | all-to-all | bytes 524288 | tf_op jit(solution)/shard_map/all_to_all | solution.py:177
  (101 shorter events, 37.4 us)
Async XLA Ops:
  6.5 134.2 %copy-start = (f32[32,8]{0,1:T(8,128)S(1)}, f32[32,8]{0,1:T(8,128)}, u32[]{:S(2)}) copy-start(f32[32,8]{0,1:T(8,128)} %param.26) | copy-start | bytes 3076
  6.5 110.2 %all-gather.2.cloned.1.call-start = ((), (), s32[]{:S(2)}) async-start(), calls=%async_computation.6 | async-start | bytes 8519680 | tf_op jit(solution)/shard_map/all_gather | solution.py:103
  9.6 15.0 %copy-start.10 = (s32[64,1]{0,1:T(1,128)S(1)}, s32[64,1]{0,1:T(1,128)}, u32[]{:S(2)}) copy-start(s32[64,1]{0,1:T(1,128)} %param.17) | copy-start | bytes 772
  9.6 69.6 %copy-start.4 = (bf16[64,1024]{1,0:T(8,128)(2,1)S(1)}, bf16[64,1024]{1,0:T(8,128)(2,1)}, u32[]{:S(2)}) copy-start(bf16[64,1024]{1,0:T(8,128)(2,1)} %param.16) | copy-start | bytes 393220
  9.6 69.6 %copy-start.5 = (f32[1024]{0:T(1024)S(1)}, f32[1024]{0:T(1024)}, u32[]{:S(2)}) copy-start(f32[1024]{0:T(1024)} %param.20) | copy-start | bytes 12292
  9.6 69.6 %all-to-all-start.1 = ((bf16[64,16,1024]{2,1,0:T(8,128)(2,1)}), bf16[64,16,1024]{2,1,0:T(8,128)(2,1)S(1)}, u32[]{:S(2)}, u32[]{:S(2)}) async-start(bf16[64,16,1024]{2,1,0:T(8,128)(2,1)} %broadcast_in_dim.96), calls=%async_computation.1 | async-start | bytes 4194304 | tf_op jit(solution)/shard_map/all_to_all | solution.py:12
  24.6 63.1 %copy-start.11 = (s32[64]{0:T(128)S(1)}, s32[64]{0:T(128)}, u32[]{:S(2)}) copy-start(s32[64]{0:T(128)} %param.18) | copy-start | bytes 772
  24.8 91.9 %copy-start.7 = (s32[64]{0:T(128)}, s32[64]{0:T(128)S(1)}, u32[]{:S(2)}) copy-start(s32[64]{0:T(128)S(1)} %multiply_add_fusion) | copy-start | bytes 772
  80.7 22.4 %all-to-all-start.2 = ((bf16[64,2,1024]{2,1,0:T(2,128)(2,1)}), bf16[64,2,1024]{2,1,0:T(2,128)(2,1)S(1)}, u32[]{:S(2)}, u32[]{:S(2)}) async-start(bf16[64,2,1024]{2,1,0:T(2,128)(2,1)} %reshape.196), calls=%async_computation.2 | async-start | bytes 524288 | tf_op jit(solution)/shard_map/all_to_all | solution.py:90
  103.1 19.4 %all-to-all-start = ((bf16[64,1,2]{2,1,0:T(2,128)(2,1)}), bf16[64,1,2]{2,1,0:T(2,128)(2,1)S(1)}, u32[]{:S(2)}, u32[]{:S(2)}) async-start(bf16[64,1,2]{2,1,0:T(2,128)(2,1)} %convert_element_type.88), calls=%async_computation | async-start | bytes 65536 | tf_op jit(solution)/shard_map/all_to_all | solution.py:97
  121.5 1.0 copy-start.1
  124.2 55.1 %all-to-all-start.3 = ((bf16[8,128,1024]{2,1,0:T(8,128)(2,1)}), bf16[8,128,1024]{2,1,0:T(8,128)(2,1)}, u32[]{:S(2)}, u32[]{:S(2)}) async-start(bf16[8,128,1024]{2,1,0:T(8,128)(2,1)} %stack.2), calls=%async_computation.3 | async-start | bytes 4194304 | tf_op jit(solution)/shard_map/all_to_all | solution.py:160
  136.8 3.9 %copy-start.9 = (s32[1,1024]{1,0:T(1,128)S(1)}, s32[1,1024]{1,0:T(1,128)}, u32[]{:S(2)}) copy-start(s32[1,1024]{1,0:T(1,128)} %param.25) | copy-start | bytes 12292
  179.3 3.4 %copy-start.2 = (bf16[128,8,128]{2,0,1:T(8,128)(2,1)}, bf16[128,8,128]{2,0,1:T(8,128)(2,1)S(1)}, u32[]{:S(2)}) copy-start(bf16[128,8,128]{2,0,1:T(8,128)(2,1)S(1)} %get-tuple-element.743) | copy-start | bytes 786436 | tf_op jit(solution)/shard_map/while
  203.6 1.1 copy-start.3
  204.7 3.4 %copy-start.2 = (bf16[128,8,128]{2,0,1:T(8,128)(2,1)}, bf16[128,8,128]{2,0,1:T(8,128)(2,1)S(1)}, u32[]{:S(2)}) copy-start(bf16[128,8,128]{2,0,1:T(8,128)(2,1)S(1)} %get-tuple-element.743) | copy-start | bytes 786436 | tf_op jit(solution)/shard_map/while
  229.0 1.1 copy-start.3
  283.0 0.7 copy-start.6
  283.5 24.5 %copy-start.8 = (s32[64]{0:T(128)S(1)}, s32[64]{0:T(128)}, u32[]{:S(2)}) copy-start(s32[64]{0:T(128)} %copy-done.7) | copy-start | bytes 772
Sparse Core Ops, SparseCore 0:
  10.7 105.9 all-gather.1
